TPU v7x, 32 devices: a whole 2x2x4 slice. The times are simulated.
32 devices in a mesh: energy: 8 (over z, y), atoms: 4 (over x, core).
Axes of the slice: x: 2, y: 2, z: 4, core: 2. Of those that a mesh axis runs over, the one named last changes fastest.
Arguments:
- green: bfloat16 [1024, 32, 288], P('energy', 'atoms'), may hold values from -6 to 6
- superop: bfloat16 [4, 288, 288], replicated, may hold values from -0.1875 to 0.1875
- phonon: bfloat16 [8, 2048], replicated, may hold values from -0.1875 to 0.1875
- owner: int32 [32, 1], P('atoms'), may hold values from 0 to 7; in each aligned block of 8 rows (0 to 7, 8 to 15, ...) at most 4 rows name the same one
- neighbours: int32 [32, 4], P('atoms'), may hold values from -1 to 31, as said below
Outputs:
- self_energy: bfloat16 [1024, 32, 288], P('energy', 'atoms')
Inputs may be any that keep to these rules, and one draw needn't show every extreme that they name: `owner`: within each aligned block of 8 atoms (one atom group) no domain holds more than 4 atoms, and some domain holds exactly 4. `neighbours`: each entry is -1 or the index of an atom at most 8 away from the row's atom; some entry lies exactly 8 above its row's atom, in the next atom group.
All inputs are finite; a program needn't handle non-finite values.
Results may differ from a plain program's by a relative error of at most 0.0049.
Values may be sent and summed in bfloat16 or wider, within the bound.
A program may use at most 64 MiB of HBM per device.

v0:
```python
import jax
import jax.numpy as jnp
from jax import lax
from jax.sharding import PartitionSpec as P

SPLIT = 2
HALO = 8
ATOMS_DEV = 1


def padded(block, sides, width):
    for axis, dim in sides:
        count = lax.axis_size(axis)
        forward = [(i, i + 1) for i in range(count - 1)]
        backward = [(target, source) for source, target in forward]
        low = lax.ppermute(
            lax.slice_in_dim(block, block.shape[dim] - width, None, axis=dim), axis, forward
        )
        high = lax.ppermute(lax.slice_in_dim(block, 0, width, axis=dim), axis, backward)
        block = jnp.concatenate([low, block, high], axis=dim)
    return block


def toeplitz_rows(kernel_row, count):
    length = 2 * count
    flipped = kernel_row[::-1]
    tiled = jnp.tile(flipped, count)[: count * (length - 1)]
    return tiled.reshape(count, length - 1)[:, count - 1 : 2 * count - 1]


def per_device(green, superop, phonon, owner, neighbours):
    local_energies = green.shape[0]
    group_size = green.shape[1]
    comps = green.shape[2]
    slots = neighbours.shape[1]
    half_width = comps // SPLIT
    group = lax.axis_index("atoms")
    widened = padded(green, (("atoms", 1),), HALO)
    present = neighbours >= 0
    target_rows = jnp.where(present, neighbours - group * group_size + HALO, 0)
    picked = jnp.take(widened, target_rows.reshape(-1), axis=1)
    picked = jnp.where(present.reshape(1, -1, 1), picked, jnp.zeros_like(picked))
    coupled = jnp.dot(
        picked.reshape(local_energies * group_size, slots * comps),
        superop.reshape(slots * comps, comps),
        preferred_element_type=jnp.float32,
    )
    coupled = coupled.reshape(local_energies, group_size, comps).astype(jnp.bfloat16)
    count = local_energies * lax.axis_size("energy")
    energy_rank = lax.axis_index("energy")
    first_atom = energy_rank * ATOMS_DEV
    mine = lax.dynamic_slice_in_dim(owner[:, 0], first_atom, ATOMS_DEV)

    def build_kernel(domain):
        return toeplitz_rows(phonon[domain], count)

    kernels = jax.vmap(build_kernel)(mine)
    split_blocks = coupled.reshape(local_energies, group_size, SPLIT, half_width)
    product = jnp.einsum(
        "oph,hoiw->poiw",
        kernels,
        lax.all_to_all(split_blocks, "energy", split_axis=1, concat_axis=0, tiled=True),
        preferred_element_type=jnp.float32,
    )
    result = lax.all_to_all(
        product.astype(jnp.bfloat16), "energy", split_axis=0, concat_axis=1, tiled=True
    )
    result = result.reshape(local_energies, group_size, comps)
    return result


def solution(mesh):
    return jax.shard_map(
        per_device,
        mesh=mesh,
        in_specs=(P("energy", "atoms", None), P(), P(), P("atoms", None), P("atoms", None)),
        out_specs=P("energy", "atoms", None),
        check_vma=False,
    )
```

profile of v0, /device:TPU:1, one launch (start us, length us, event | category | flops | bytes accessed | tf_op | source)
XLA Modules:
  0.0 189.6 jit_solution(14059286615766283664)
XLA Ops:
  0.0 0.0 copy-start
  0.0 4.6 %collective-permute-start = (bf16[128,8,288]{0,2,1:T(8,128)(2,1)}, bf16[128,8,288]{0,2,1:T(8,128)(2,1)S(1)}, u32[]{:S(2)}, u32[]{:S(2)}) collective-permute-start(bf16[128,8,288]{0,2,1:T(8,128)(2,1)} %param.5), channel_id=1, source_target_pairs={{0,1},{1,2},{2,3},{4,5},{5,6},{6,7},{8,9},{9,10},{10,11},{12,13},{... | collective-permute-start | bytes 1769480 | tf_op jit(solution)/shard_map/ppermute | solution.py:16
  4.6 1.9 %collective-permute-start.1 = (bf16[128,8,288]{0,2,1:T(8,128)(2,1)}, bf16[128,8,288]{0,2,1:T(8,128)(2,1)}, u32[]{:S(2)}, u32[]{:S(2)}) collective-permute-start(bf16[128,8,288]{0,2,1:T(8,128)(2,1)} %param.5), channel_id=1, source_target_pairs={{1,0},{2,1},{3,2},{5,4},{6,5},{7,6},{9,8},{10,9},{11,10},{13,12},{... | collective-permute-start | bytes 1769480 | tf_op jit(solution)/shard_map/ppermute | solution.py:19
  6.6 1.2 constant_dynamic-slice_fusion.1
  9.8 0.8 constant_dynamic-slice_fusion
  10.5 1.5 reverse
  12.0 0.5 broadcast_bitcast_fusion
  12.6 0.0 copy-start.3
  12.6 0.0 copy-start.1
  12.6 24.7 %copy.31 = bf16[1,1,1024,2048]{3,1,2,0:T(2,128)(2,1)} copy(bf16[1,1,1024,2048]{3,2,1,0:T(8,128)(2,1)S(1)} %broadcast_bitcast_fusion) | data formatting | bytes 8388608
  37.2 0.0 copy-done.3
  37.3 0.1 copy.22
  37.3 0.1 reshape.125
  37.4 0.1 copy.20
  37.5 0.1 broadcast_in_dim.34
  37.6 0.1 copy.21
  37.7 0.1 broadcast_in_dim.37
  37.9 0.0 collective-permute-done
  37.9 0.0 copy-start.2
  37.9 0.8 copy-done.2
  38.7 0.0 collective-permute-done.1
  38.7 0.0 copy-done.1
  38.7 1.4 pad_maximum_fusion
  40.1 2.3 %gather_fusion = bf16[32,128,288]{1,2,0:T(8,128)(2,1)} fusion(bf16[128,24,288]{0,2,1:T(8,128)(2,1)S(1)} %pad_maximum_fusion, s32[1024]{0:T(1024)S(1)} %pad_clamp_fusion), kind=kCustom, calls=%fused_computation | custom fusion | bytes 4718720 | tf_op jit(solution)/shard_map/jit(_take)/gather | solution.py:41
  42.5 7.8 %select_select_fusion = bf16[32,128,288]{1,2,0:T(8,128)(2,1)S(1)} fusion(bf16[32,128,288]{1,2,0:T(8,128)(2,1)} %gather_fusion, pred[32,288]{1,0:T(8,128)(4,1)S(1)} %broadcast_in_dim.35, pred[32,288]{1,0:T(8,128)(4,1)S(1)} %broadcast_in_dim.38), kind=kLoop, calls=%fused_computation.2 | loop fusion | flops 2359296 | bytes 4737024 | tf_op jit(solution)/shard_map/jit(_where)/select_n | solution.py:42
  50.3 0.0 copy-done
  50.3 1.8 convolution_convert_fusion
  52.1 5.6 %all-to-all-start = ((bf16[128,8,2,144]{0,3,2,1:T(8,128)(2,1)}), bf16[128,8,2,144]{0,3,2,1:T(8,128)(2,1)S(1)}, u32[]{:S(2)}, u32[]{:S(2)}) async-start(bf16[128,8,2,144]{0,3,2,1:T(8,128)(2,1)} %bitcast.5), calls=%async_computation | async-start | bytes 1179648 | tf_op jit(solution)/shard_map/all_to_all | solution.py:62
  57.6 84.7 %slice_reduce_fusion = bf16[2096128]{0:T(1024)(128)(2,1)} fusion(bf16[1,2097152]{1,0:T(2,128)(2,1)} %bitcast.42), kind=kLoop, calls=%fused_computation.1 | loop fusion | bytes 8384512 | tf_op jit(solution)/shard_map/vmap()/slice | solution.py:27
  142.4 10.7 %reshape.129 = bf16[1,1024,2047]{2,1,0:T(8,128)(2,1)} reshape(bf16[2096128]{0:T(1024)(128)(2,1)} %slice_reduce_fusion) | data formatting | bytes 8384512 | tf_op jit(solution)/shard_map/vmap()/reshape | solution.py:28
  153.0 0.0 all-to-all-done
  153.0 0.2 copy.25
  153.3 0.3 reshape.128
  153.5 2.7 %fusion.2 = bf16[1024,1,2,144]{0,3,2,1:T(8,128)(2,1)S(1)} fusion(bf16[1024,2,144]{0,2,1:T(8,128)(2,1)S(1)} %reshape.128, bf16[1,1024,2047]{2,1,0:T(8,128)(2,1)} %reshape.129), kind=kOutput, calls=%fused_computation.9 | convolution fusion | flops 604274688 | bytes 3276800 | tf_op jit(solution)/shard_map/oph,hoiw->poiw/dot_general | solution.py:59
  156.2 0.9 copy.26
  157.1 30.7 %all_to_all.30 = bf16[1024,1,2,144]{3,2,1,0:T(2,128)(2,1)S(1)} all-to-all(bf16[1024,1,2,144]{3,2,1,0:T(2,128)(2,1)S(1)} %copy.26), channel_id=1, replica_groups=mesh['energy'=8,'atoms'=4] {'energy'}, dimensions={0} | all-to-all | bytes 1179648 | tf_op jit(solution)/shard_map/all_to_all | solution.py:65
  187.8 1.8 copy.27
  (6 shorter events, 0.1 us)
Async XLA Ops:
  0.0 50.3 %copy-start = (bf16[4,288,288]{2,1,0:T(8,128)(2,1)S(1)}, bf16[4,288,288]{2,1,0:T(8,128)(2,1)}, u32[]{:S(2)}) copy-start(bf16[4,288,288]{2,1,0:T(8,128)(2,1)} %param.6) | copy-start | bytes 1990660
  0.0 37.9 %collective-permute-start = (bf16[128,8,288]{0,2,1:T(8,128)(2,1)}, bf16[128,8,288]{0,2,1:T(8,128)(2,1)S(1)}, u32[]{:S(2)}, u32[]{:S(2)}) collective-permute-start(bf16[128,8,288]{0,2,1:T(8,128)(2,1)} %param.5), channel_id=1, source_target_pairs={{0,1},{1,2},{2,3},{4,5},{5,6},{6,7},{8,9},{9,10},{10,11},{12,13},{... | collective-permute-start | bytes 1769480 | tf_op jit(solution)/shard_map/ppermute | solution.py:16
  4.6 34.0 %collective-permute-start.1 = (bf16[128,8,288]{0,2,1:T(8,128)(2,1)}, bf16[128,8,288]{0,2,1:T(8,128)(2,1)}, u32[]{:S(2)}, u32[]{:S(2)}) collective-permute-start(bf16[128,8,288]{0,2,1:T(8,128)(2,1)} %param.5), channel_id=1, source_target_pairs={{1,0},{2,1},{3,2},{5,4},{6,5},{7,6},{9,8},{10,9},{11,10},{13,12},{... | collective-permute-start | bytes 1769480 | tf_op jit(solution)/shard_map/ppermute | solution.py:19
  12.6 24.7 %copy-start.3 = (s32[8,4]{0,1:T(4,128)S(1)}, s32[8,4]{0,1:T(4,128)}, u32[]{:S(2)}) copy-start(s32[8,4]{0,1:T(4,128)} %param.9) | copy-start | bytes 388
  12.6 26.1 %copy-start.1 = (bf16[128,8,288]{0,2,1:T(8,128)(2,1)S(1)}, bf16[128,8,288]{0,2,1:T(8,128)(2,1)}, u32[]{:S(2)}) copy-start(bf16[128,8,288]{0,2,1:T(8,128)(2,1)} %param.5) | copy-start | bytes 1769476
  37.9 0.8 copy-start.2
  52.1 101.0 %all-to-all-start = ((bf16[128,8,2,144]{0,3,2,1:T(8,128)(2,1)}), bf16[128,8,2,144]{0,3,2,1:T(8,128)(2,1)S(1)}, u32[]{:S(2)}, u32[]{:S(2)}) async-start(bf16[128,8,2,144]{0,3,2,1:T(8,128)(2,1)} %bitcast.5), calls=%async_computation | async-start | bytes 1179648 | tf_op jit(solution)/shard_map/all_to_all | solution.py:62
where the time goes:
time: 190 us
  local copies, waits for them, and re-layouts  131 us (69%)
  blocking collectives  30.7 us (16%)
  starting transfers between devices  12.1 us (6%)
  other arithmetic  9.3 us (5%)
  matrix products  4.5 us (2%)
  between operations  2.1 us (1%)
    slice x1, local copies, waits for them, and re-layouts, toeplitz_rows(): tiled = jnp.tile(flipped, count)[:count * (length - 1)]  84.7 us
    all_to_all x1, blocking collectives, per_device(): lax.all_to_all(product.astype(jnp.bfloat16), 'energy', split_axis=0, conc...  30.7 us
    unnamed x11, local copies, waits for them, and re-layouts  27.5 us
    reshape x1, local copies, waits for them, and re-layouts, toeplitz_rows(): return tiled.reshape(count, length - 1)[:, count - 1:2 * count - 1]  10.7 us
    select_n x1, other arithmetic, per_device(): jnp.where(present.reshape(1, -1, 1), picked, jnp.zeros_like(picked))  7.81 us
    all_to_all x1, starting transfers between devices, per_device(): lax.all_to_all(split_blocks, 'energy', split_axis=1, concat_axis=0, tiled...  5.55 us
    ppermute x1, starting transfers between devices, padded(): lax.ppermute(lax.slice_in_dim(block, block.shape[dim] - width, None, axis...  4.63 us
  transfers between devices with their start and end apart: 3, of which 0 were waited for; matrix products, arithmetic and copies ran while one was open for 66% of the time, Pallas kernels for 0%

commit v1 on v0

v1 whole, which is shorter than its diff:
```python
import functools

import jax
import jax.numpy as jnp
from jax import lax
from jax.experimental import pallas as pl
from jax.experimental.pallas import tpu as pltpu
from jax.sharding import PartitionSpec as P

HALO = 8
MESH = pl.DeviceIdType.MESH
F32 = jnp.float32
BF16 = jnp.bfloat16


def chunks_of(comps, step=128):
    return [(at, min(step, comps - at)) for at in range(0, comps, step)]


def dot(a, b):
    return jnp.dot(a, b, preferred_element_type=F32)


def kernel(
    parts, groups,
    green, superop, phonon, owner, neighbours,
    out,
    wide, turned, table, sent, held, back,
    own_sem, halo_send, halo_recv, go_send, go_recv, ret_send, ret_recv,
):
    me = lax.axis_index("energy")
    group = lax.axis_index("atoms")
    has_left, has_right = group > 0, group < groups - 1
    atoms, comps, local = green.shape
    each = atoms // parts
    slots = neighbours.shape[0]
    span = phonon.shape[1]
    count = span // 2
    deep = table.shape[1]
    per = deep // local
    pieces = chunks_of(comps)

    barrier = pltpu.get_barrier_semaphore()
    for step in range(1, parts):
        peer = lax.rem(me + step, parts)
        pl.semaphore_signal(barrier, inc=1, device_id=(peer, group), device_id_type=MESH)

    @pl.when(has_left)
    def _():
        pl.semaphore_signal(barrier, inc=1, device_id=(me, group - 1), device_id_type=MESH)

    @pl.when(has_right)
    def _():
        pl.semaphore_signal(barrier, inc=1, device_id=(me, group + 1), device_id_type=MESH)

    own = pltpu.make_async_copy(green, wide.at[pl.ds(HALO, atoms)], own_sem)
    own.start()
    pl.semaphore_wait(barrier, parts - 1 + jnp.where(has_left, 1, 0) + jnp.where(has_right, 1, 0))

    to_left = pltpu.make_async_remote_copy(
        src_ref=green.at[pl.ds(0, HALO)], dst_ref=wide.at[pl.ds(HALO + atoms, HALO)],
        send_sem=halo_send.at[0], recv_sem=halo_recv.at[0],
        device_id=(me, group - 1), device_id_type=MESH)
    to_right = pltpu.make_async_remote_copy(
        src_ref=green.at[pl.ds(atoms - HALO, HALO)], dst_ref=wide.at[pl.ds(0, HALO)],
        send_sem=halo_send.at[1], recv_sem=halo_recv.at[1],
        device_id=(me, group + 1), device_id_type=MESH)

    @pl.when(has_left)
    def _():
        to_left.start()

    @pl.when(has_right)
    def _():
        to_right.start()

    empty = 2 * HALO + atoms
    wide[empty] = jnp.zeros((comps, local), BF16)
    turned[...] = superop[...].astype(F32).T.astype(BF16)

    for mine in range(each):
        domain = owner[0, me * each + mine]
        named = lax.broadcasted_iota(jnp.int32, phonon.shape, 0) == domain
        line = jnp.sum(jnp.where(named, phonon[...].astype(F32), 0.0), axis=0, keepdims=True)
        first = pltpu.roll(jnp.broadcast_to(line, (8, span)), 0, 1, stride=1, stride_axis=0)
        for at in range(0, deep, 16):
            pair = [pltpu.roll(first, at, 1) if at else first, pltpu.roll(first, at + 8, 1)]
            table[mine, at:at + 16, :] = jnp.concatenate(pair, axis=0).astype(BF16)

    own.wait()

    @pl.when(has_right)
    def _():
        to_left.wait_recv()

    @pl.when(has_left)
    def _():
        to_right.wait_recv()

    def place(atom, slot):
        target = neighbours[slot, atom]
        near = jnp.clip(target - group * atoms + HALO, 0, empty)
        return jnp.where(target >= 0, near, empty)

    def couple(pair, carry):
        picked = jnp.concatenate([
            jnp.concatenate(
                [wide[place(2 * pair, slot)], wide[place(2 * pair + 1, slot)]], axis=1)
            for slot in range(slots)], axis=0)
        total = dot(turned[...], picked).astype(BF16)
        sent[2 * pair] = total[:, :local]
        sent[2 * pair + 1] = total[:, local:]
        return carry

    lax.fori_loop(0, atoms // 2, couple, 0)

    def go(chunk, step):
        at, size = pieces[chunk]
        peer = lax.rem(me + step, parts)
        return pltpu.make_async_remote_copy(
            src_ref=sent.at[pl.ds(peer * each, each), pl.ds(at, size)],
            dst_ref=held.at[pl.ds(me * each, each), pl.ds(at, size)],
            send_sem=go_send.at[chunk, step], recv_sem=go_recv.at[chunk, step],
            device_id=(peer, group), device_id_type=MESH,
        )

    def ret(chunk, step):
        at, size = pieces[chunk]
        peer = lax.rem(me + step, parts)
        return pltpu.make_async_remote_copy(
            src_ref=back.at[pl.ds(peer * each, each), pl.ds(at, size)],
            dst_ref=out.at[pl.ds(me * each, each), pl.ds(at, size)],
            send_sem=ret_send.at[chunk, step], recv_sem=ret_recv.at[chunk, step],
            device_id=(peer, group), device_id_type=MESH,
        )

    for chunk in range(len(pieces)):
        for step in range(1, parts):
            go(chunk, step).start()
    here = pl.ds(me * each, each)
    held[here] = sent[here]

    for chunk, (at, size) in enumerate(pieces):
        for step in range(1, parts):
            go(chunk, step).wait_recv()
        for mine in range(each):
            total = jnp.zeros((size, count), F32)
            for depth in range(count // deep):
                columns = jnp.concatenate(
                    [held[(depth * per + i) * each + mine, at:at + size, :] for i in range(per)],
                    axis=1)
                first = count - deep * depth
                total = total + dot(columns, table[mine, :, first:first + count])
            total = total.astype(BF16)
            for part in range(parts):
                back[part * each + mine, at:at + size, :] = total[:, part * local:(part + 1) * local]
        for step in range(1, parts):
            ret(chunk, step).start()
        out[here, at:at + size, :] = back[here, at:at + size, :]

    @pl.when(has_left)
    def _():
        to_left.wait_send()

    @pl.when(has_right)
    def _():
        to_right.wait_send()

    for chunk in range(len(pieces)):
        for step in range(1, parts):
            go(chunk, step).wait_send()
    for chunk in range(len(pieces)):
        for step in range(1, parts):
            ret(chunk, step).wait()


def solution(mesh):
    parts, groups = mesh.shape["energy"], mesh.shape["atoms"]

    def per_device(green, superop, phonon, owner, neighbours):
        local, atoms, comps = green.shape
        slots = neighbours.shape[1]
        pieces = len(chunks_of(comps))
        vmem, smem = pl.BlockSpec(memory_space=pltpu.VMEM), pl.BlockSpec(memory_space=pltpu.SMEM)
        result = pl.pallas_call(
            functools.partial(kernel, parts, groups),
            out_shape=jax.ShapeDtypeStruct((atoms, comps, local), BF16),
            in_specs=[pl.BlockSpec(memory_space=pl.ANY), vmem, vmem, smem, smem],
            out_specs=vmem,
            scratch_shapes=[
                pltpu.VMEM((atoms + 2 * HALO + 1, comps, local), BF16),
                pltpu.VMEM((comps, slots * comps), BF16),
                pltpu.VMEM((atoms // parts, 2 * local, phonon.shape[1]), BF16),
                pltpu.VMEM((atoms, comps, local), BF16),
                pltpu.VMEM((atoms, comps, local), BF16),
                pltpu.VMEM((atoms, comps, local), BF16),
                pltpu.SemaphoreType.DMA,
                pltpu.SemaphoreType.DMA((2,)),
                pltpu.SemaphoreType.DMA((2,)),
                pltpu.SemaphoreType.DMA((pieces, parts)),
                pltpu.SemaphoreType.DMA((pieces, parts)),
                pltpu.SemaphoreType.DMA((pieces, parts)),
                pltpu.SemaphoreType.DMA((pieces, parts)),
            ],
            compiler_params=pltpu.CompilerParams(
                collective_id=0, has_side_effects=True, vmem_limit_bytes=48 * 1024 * 1024
            ),
        )(jnp.transpose(green, (1, 2, 0)), superop.reshape(slots * comps, comps), phonon,
          owner.T, neighbours.T)
        return jnp.transpose(result, (2, 0, 1))

    return jax.shard_map(
        per_device,
        mesh=mesh,
        in_specs=(P("energy", "atoms", None), P(), P(), P("atoms", None), P("atoms", None)),
        out_specs=P("energy", "atoms", None),
        check_vma=False,
    )
```

time: 190 us -> 43 us (0.23)
  local copies, waits for them, and re-layouts: 131 us -> 4.49 us
  Pallas kernels: 0 us -> 38.2 us
  blocking collectives: 30.7 us -> 0 us
  starting transfers between devices: 12.1 us -> 0 us
  other arithmetic: 9.3 us -> 0 us
  matrix products: 4.5 us -> 0 us
  between operations: 2.1 us -> 0.01 us
    slice x1 -> x0, local copies, waits for them, and re-layouts: 84.7 us -> none  [toeplitz_rows(): tiled = jnp.tile(flipped, count)[:count * (length - 1)]]
    pallas_call x0 -> x1, Pallas kernels: none -> 38.2 us  [per_device(): pl.pallas_call(functools.partial(kernel, parts, groups), out_shape=jax.Sh...]
    all_to_all x1 -> x0, blocking collectives: 30.7 us -> none  [per_device(): lax.all_to_all(product.astype(jnp.bfloat16), 'energy', split_axis=0, conc...]
    unnamed x11, local copies, waits for them, and re-layouts: 27.5 us -> 4.49 us
    reshape x2 -> x0, local copies, waits for them, and re-layouts: 10.7 us -> none  [the longest x1 10.7 us: toeplitz_rows(): return tiled.reshape(count, length - 1)[:, count - 1:2 * count - 1]]
    select_n x2 -> x0, other arithmetic: 7.82 us -> none  [the longest x1 7.81 us: per_device(): jnp.where(present.reshape(1, -1, 1), picked, jnp.zeros_like(picked))]
    ppermute x2 -> x0, starting transfers between devices: 6.55 us -> none  [the longest x1 4.63 us: padded(): lax.ppermute(lax.slice_in_dim(block, block.shape[dim] - width, None, axis...]
    all_to_all x1 -> x0, starting transfers between devices: 5.55 us -> none  [per_device(): lax.all_to_all(split_blocks, 'energy', split_axis=1, concat_axis=0, tiled...]
  transfers between devices with their start and end apart: 3 -> 0, of which waited for: 0 -> 0; matrix products, arithmetic and copies ran while one was open for 66% -> 0% of each run, Pallas kernels for 0% -> 0%
where the time goes in v1:
time: 43 us; the launch traced here: 42.7 us
  Pallas kernels  38.2 us (89%)
  local copies, waits for them, and re-layouts  4.49 us (10%)
    pallas_call x1, Pallas kernels, per_device(): pl.pallas_call(functools.partial(kernel, parts, groups), out_shape=jax.Sh...  38.2 us
    unnamed x11, local copies, waits for them, and re-layouts  4.49 us

profile of v1, /device:TPU:1, one launch (start us, length us, event | category | flops | bytes accessed | tf_op | source)
XLA Modules:
  0.0 42.7 jit_solution(138807191710275041)
XLA Ops:
  0.0 0.0 copy-start.3
  0.0 0.0 copy-start.4
  0.0 0.7 %copy-done.3 = s32[8,4]{0,1:T(4,128)S(1)} copy-done((s32[8,4]{0,1:T(4,128)S(1)}, s32[8,4]{0,1:T(4,128)}, u32[]{:S(2)}) %copy-start.3) | copy-done | bytes 152
  0.7 0.0 copy-done.4
  0.7 0.0 copy-start
  0.7 1.2 %copy-done = bf16[4,288,288]{2,1,0:T(8,128)(2,1)S(1)} copy-done((bf16[4,288,288]{2,1,0:T(8,128)(2,1)S(1)}, bf16[4,288,288]{2,1,0:T(8,128)(2,1)}, u32[]{:S(2)}) %copy-start) | copy-done | bytes 663576
  1.9 0.0 copy-start.1
  1.9 1.1 %copy-done.1 = bf16[128,8,288]{0,2,1:T(8,128)(2,1)S(1)} copy-done((bf16[128,8,288]{0,2,1:T(8,128)(2,1)S(1)}, bf16[128,8,288]{0,2,1:T(8,128)(2,1)}, u32[]{:S(2)}) %copy-start.1) | copy-done | bytes 589848
  2.9 0.0 copy-start.2
  2.9 0.8 %copy-done.2 = bf16[8,2048]{1,0:T(8,128)(2,1)S(1)} copy-done((bf16[8,2048]{1,0:T(8,128)(2,1)S(1)}, bf16[8,2048]{1,0:T(8,128)(2,1)}, u32[]{:S(2)}) %copy-start.2) | copy-done | bytes 32792
  3.7 38.2 %shard_map.55 = bf16[8,288,128]{2,1,0:T(8,128)(2,1)S(1)} custom-call(bf16[8,288,128]{2,1,0:T(8,128)(2,1)S(1)} %bitcast.7, bf16[1152,288]{1,0:T(8,128)(2,1)S(1)} %bitcast.6, bf16[8,2048]{1,0:T(8,128)(2,1)S(1)} %copy-done.2, s32[1,8]{1,0:T(1,128)S(1)} %bitcast.9, s32[4,8]{1,0:T(4,128)S(1)} %bitcast.8), custom_call_target="tpu_custom_call" | custom-call | tf_op jit(solution)/shard_map/pallas_call | solution.py:185
  41.8 0.8 %copy.7 = bf16[128,8,288]{0,2,1:T(8,128)(2,1)} copy(bf16[128,8,288]{0,2,1:T(8,128)(2,1)S(1)} %bitcast.5) | data formatting | bytes 1179648
Async XLA Ops:
  0.0 0.7 %copy-start.3 = (s32[8,4]{0,1:T(4,128)S(1)}, s32[8,4]{0,1:T(4,128)}, u32[]{:S(2)}) copy-start(s32[8,4]{0,1:T(4,128)} %param.9) | copy-start | bytes 388
  0.0 0.7 %copy-start.4 = (s32[8,1]{0,1:T(1,128)S(1)}, s32[8,1]{0,1:T(1,128)}, u32[]{:S(2)}) copy-start(s32[8,1]{0,1:T(1,128)} %param.8) | copy-start | bytes 100
  0.7 1.2 %copy-start = (bf16[4,288,288]{2,1,0:T(8,128)(2,1)S(1)}, bf16[4,288,288]{2,1,0:T(8,128)(2,1)}, u32[]{:S(2)}) copy-start(bf16[4,288,288]{2,1,0:T(8,128)(2,1)} %param.6) | copy-start | bytes 1990660
  1.9 1.1 %copy-start.1 = (bf16[128,8,288]{0,2,1:T(8,128)(2,1)S(1)}, bf16[128,8,288]{0,2,1:T(8,128)(2,1)}, u32[]{:S(2)}) copy-start(bf16[128,8,288]{0,2,1:T(8,128)(2,1)} %param.5) | copy-start | bytes 1769476
  2.9 0.8 %copy-start.2 = (bf16[8,2048]{1,0:T(8,128)(2,1)S(1)}, bf16[8,2048]{1,0:T(8,128)(2,1)}, u32[]{:S(2)}) copy-start(bf16[8,2048]{1,0:T(8,128)(2,1)} %phonon.1) | copy-start | bytes 98308

commit v2 on v1

--- a/solution.py
+++ b/solution.py
@@ -23,10 +23,10 @@
 
 def kernel(
     parts, groups,
-    green, superop, phonon, owner, neighbours,
+    green, superop_hbm, phonon_hbm, owner_hbm, neighbours_hbm,
     out,
-    wide, turned, table, sent, held, back,
-    own_sem, halo_send, halo_recv, go_send, go_recv, ret_send, ret_recv,
+    superop, phonon, owner, neighbours, wide, turned, table, sent, held, back,
+    own_sem, load_sem, halo_send, halo_recv, go_send, go_recv, ret_send, ret_recv,
 ):
     me = lax.axis_index("energy")
     group = lax.axis_index("atoms")
@@ -40,6 +40,15 @@
     per = deep // local
     pieces = chunks_of(comps)
 
+    loads = [
+        pltpu.make_async_copy(source, target, load_sem.at[i])
+        for i, (source, target) in enumerate([
+            (superop_hbm, superop), (phonon_hbm, phonon), (owner_hbm, owner),
+            (neighbours_hbm, neighbours)])
+    ]
+    for load in loads:
+        load.start()
+
     barrier = pltpu.get_barrier_semaphore()
     for step in range(1, parts):
         peer = lax.rem(me + step, parts)
@@ -76,6 +85,8 @@
 
     empty = 2 * HALO + atoms
     wide[empty] = jnp.zeros((comps, local), BF16)
+    for load in loads:
+        load.wait()
     turned[...] = superop[...].astype(F32).T.astype(BF16)
 
     for mine in range(each):
@@ -101,18 +112,6 @@
         target = neighbours[slot, atom]
         near = jnp.clip(target - group * atoms + HALO, 0, empty)
         return jnp.where(target >= 0, near, empty)
-
-    def couple(pair, carry):
-        picked = jnp.concatenate([
-            jnp.concatenate(
-                [wide[place(2 * pair, slot)], wide[place(2 * pair + 1, slot)]], axis=1)
-            for slot in range(slots)], axis=0)
-        total = dot(turned[...], picked).astype(BF16)
-        sent[2 * pair] = total[:, :local]
-        sent[2 * pair + 1] = total[:, local:]
-        return carry
-
-    lax.fori_loop(0, atoms // 2, couple, 0)
 
     def go(chunk, step):
         at, size = pieces[chunk]
@@ -134,8 +133,33 @@
             device_id=(peer, group), device_id_type=MESH,
         )
 
-    for chunk in range(len(pieces)):
-        for step in range(1, parts):
+    unit = max(each, 2)
+    units = atoms // unit
+
+    def couple(turn, carry):
+        at_unit = lax.rem(me * each // unit + units // 2 + turn, units)
+        base = at_unit * unit
+        for first in range(0, unit, 2):
+            picked = jnp.concatenate([
+                jnp.concatenate(
+                    [wide[place(base + first, slot)], wide[place(base + first + 1, slot)]], axis=1)
+                for slot in range(slots)], axis=0)
+            total = dot(turned[...], picked).astype(BF16)
+            sent[base + first] = total[:, :local]
+            sent[base + first + 1] = total[:, local:]
+        for which in range(unit // each):
+            peer = at_unit * (unit // each) + which
+
+            @pl.when(peer != me)
+            def _(peer=peer):
+                go(0, lax.rem(peer - me + parts, parts)).start()
+        return carry
+
+    lax.fori_loop(0, units, couple, 0)
+
+    far_first = sorted(range(1, parts), key=lambda step: abs(step - parts // 2))
+    for chunk in range(1, len(pieces)):
+        for step in far_first:
             go(chunk, step).start()
     here = pl.ds(me * each, each)
     held[here] = sent[here]
@@ -154,7 +178,7 @@
             total = total.astype(BF16)
             for part in range(parts):
                 back[part * each + mine, at:at + size, :] = total[:, part * local:(part + 1) * local]
-        for step in range(1, parts):
+        for step in far_first:
             ret(chunk, step).start()
         out[here, at:at + size, :] = back[here, at:at + size, :]
 
@@ -181,13 +205,17 @@
         local, atoms, comps = green.shape
         slots = neighbours.shape[1]
         pieces = len(chunks_of(comps))
-        vmem, smem = pl.BlockSpec(memory_space=pltpu.VMEM), pl.BlockSpec(memory_space=pltpu.SMEM)
+        hbm = pl.BlockSpec(memory_space=pltpu.HBM)
         result = pl.pallas_call(
             functools.partial(kernel, parts, groups),
             out_shape=jax.ShapeDtypeStruct((atoms, comps, local), BF16),
-            in_specs=[pl.BlockSpec(memory_space=pl.ANY), vmem, vmem, smem, smem],
-            out_specs=vmem,
+            in_specs=[hbm] * 5,
+            out_specs=pl.BlockSpec(memory_space=pltpu.VMEM),
             scratch_shapes=[
+                pltpu.VMEM((slots * comps, comps), BF16),
+                pltpu.VMEM(phonon.shape, BF16),
+                pltpu.SMEM((1, atoms), jnp.int32),
+                pltpu.SMEM((slots, atoms), jnp.int32),
                 pltpu.VMEM((atoms + 2 * HALO + 1, comps, local), BF16),
                 pltpu.VMEM((comps, slots * comps), BF16),
                 pltpu.VMEM((atoms // parts, 2 * local, phonon.shape[1]), BF16),
@@ -195,6 +223,7 @@
                 pltpu.VMEM((atoms, comps, local), BF16),
                 pltpu.VMEM((atoms, comps, local), BF16),
                 pltpu.SemaphoreType.DMA,
+                pltpu.SemaphoreType.DMA((4,)),
                 pltpu.SemaphoreType.DMA((2,)),
                 pltpu.SemaphoreType.DMA((2,)),
                 pltpu.SemaphoreType.DMA((pieces, parts)),
@@ -203,7 +232,7 @@
                 pltpu.SemaphoreType.DMA((pieces, parts)),
             ],
             compiler_params=pltpu.CompilerParams(
-                collective_id=0, has_side_effects=True, vmem_limit_bytes=48 * 1024 * 1024
+                collective_id=0, has_side_effects=True, vmem_limit_bytes=60 * 1024 * 1024
             ),
         )(jnp.transpose(green, (1, 2, 0)), superop.reshape(slots * comps, comps), phonon,
           owner.T, neighbours.T)

time: 43 us -> 39.8 us (0.926)
  local copies, waits for them, and re-layouts: 4.49 us -> 1.92 us
    unnamed x11 -> x1, local copies, waits for them, and re-layouts: 4.49 us -> 1.92 us
where the time goes in v2:
time: 39.8 us; the launch traced here: 39.7 us
  Pallas kernels  37.8 us (95%)
  local copies, waits for them, and re-layouts  1.92 us (5%)
    pallas_call x1, Pallas kernels, per_device(): pl.pallas_call(functools.partial(kernel, parts, groups), out_shape=jax.Sh...  37.8 us
    unnamed x1, local copies, waits for them, and re-layouts  1.92 us

profile of v2, /device:TPU:1, one launch (start us, length us, event | category | flops | bytes accessed | tf_op | source)
XLA Modules:
  0.0 39.7 jit_solution(14334129474969898884)
XLA Ops:
  0.0 37.8 %shard_map.55 = bf16[8,288,128]{2,1,0:T(8,128)(2,1)} custom-call(bf16[8,288,128]{2,1,0:T(8,128)(2,1)} %bitcast.7, bf16[1152,288]{1,0:T(8,128)(2,1)} %bitcast.6, bf16[8,2048]{1,0:T(8,128)(2,1)} %phonon_hbm.1, s32[1,8]{1,0:T(1,128)} %bitcast.9, s32[4,8]{1,0:T(4,128)} %bitcast.8), custom_call_target="tpu_custom_call" | custom-call | tf_op jit(solution)/shard_map/pallas_call | solution.py:209
  37.8 1.9 %copy.7 = bf16[128,8,288]{0,2,1:T(8,128)(2,1)} copy(bf16[128,8,288]{0,2,1:T(8,128)(2,1)} %bitcast.5) | data formatting | bytes 1179648

commit v3 on v2

--- a/solution.py
+++ b/solution.py
@@ -13,7 +13,7 @@
 BF16 = jnp.bfloat16
 
 
-def chunks_of(comps, step=128):
+def chunks_of(comps, step=96):
     return [(at, min(step, comps - at)) for at in range(0, comps, step)]
 
 
@@ -89,15 +89,6 @@
         load.wait()
     turned[...] = superop[...].astype(F32).T.astype(BF16)
 
-    for mine in range(each):
-        domain = owner[0, me * each + mine]
-        named = lax.broadcasted_iota(jnp.int32, phonon.shape, 0) == domain
-        line = jnp.sum(jnp.where(named, phonon[...].astype(F32), 0.0), axis=0, keepdims=True)
-        first = pltpu.roll(jnp.broadcast_to(line, (8, span)), 0, 1, stride=1, stride_axis=0)
-        for at in range(0, deep, 16):
-            pair = [pltpu.roll(first, at, 1) if at else first, pltpu.roll(first, at + 8, 1)]
-            table[mine, at:at + 16, :] = jnp.concatenate(pair, axis=0).astype(BF16)
-
     own.wait()
 
     @pl.when(has_right)
@@ -158,11 +149,25 @@
     lax.fori_loop(0, units, couple, 0)
 
     far_first = sorted(range(1, parts), key=lambda step: abs(step - parts // 2))
+    def kept(chunk):
+        at, size = pieces[chunk]
+        here = pl.ds(me * each, each), pl.ds(at, size)
+        return pltpu.make_async_copy(back.at[here], out.at[here], ret_send.at[chunk, 0])
+
     for chunk in range(1, len(pieces)):
         for step in far_first:
             go(chunk, step).start()
     here = pl.ds(me * each, each)
     held[here] = sent[here]
+
+    for mine in range(each):
+        domain = owner[0, me * each + mine]
+        named = lax.broadcasted_iota(jnp.int32, phonon.shape, 0) == domain
+        line = jnp.sum(jnp.where(named, phonon[...].astype(F32), 0.0), axis=0, keepdims=True)
+        first = pltpu.roll(jnp.broadcast_to(line, (8, span)), 0, 1, stride=1, stride_axis=0)
+        for at in range(0, deep, 16):
+            pair = [pltpu.roll(first, at, 1) if at else first, pltpu.roll(first, at + 8, 1)]
+            table[mine, at:at + 16, :] = jnp.concatenate(pair, axis=0).astype(BF16)
 
     for chunk, (at, size) in enumerate(pieces):
         for step in range(1, parts):
@@ -180,7 +185,7 @@
                 back[part * each + mine, at:at + size, :] = total[:, part * local:(part + 1) * local]
         for step in far_first:
             ret(chunk, step).start()
-        out[here, at:at + size, :] = back[here, at:at + size, :]
+        kept(chunk).start()
 
     @pl.when(has_left)
     def _():
@@ -194,6 +199,7 @@
         for step in range(1, parts):
             go(chunk, step).wait_send()
     for chunk in range(len(pieces)):
+        kept(chunk).wait()
         for step in range(1, parts):
             ret(chunk, step).wait()
 
@@ -210,7 +216,7 @@
             functools.partial(kernel, parts, groups),
             out_shape=jax.ShapeDtypeStruct((atoms, comps, local), BF16),
             in_specs=[hbm] * 5,
-            out_specs=pl.BlockSpec(memory_space=pltpu.VMEM),
+            out_specs=hbm,
             scratch_shapes=[
                 pltpu.VMEM((slots * comps, comps), BF16),
                 pltpu.VMEM(phonon.shape, BF16),

time: 39.8 us -> 38.4 us (0.965)
  Pallas kernels: 37.8 us -> 36.3 us
    pallas_call x1, Pallas kernels: 37.8 us -> 36.3 us  [per_device(): pl.pallas_call(functools.partial(kernel, parts, groups), out_shape=jax.Sh...]
where the time goes in v3:
time: 38.4 us; the launch traced here: 38.3 us
  Pallas kernels  36.3 us (95%)
  local copies, waits for them, and re-layouts  1.92 us (5%)
    pallas_call x1, Pallas kernels, per_device(): pl.pallas_call(functools.partial(kernel, parts, groups), out_shape=jax.Sh...  36.3 us
    unnamed x1, local copies, waits for them, and re-layouts  1.92 us

profile of v3, /device:TPU:1, one launch (start us, length us, event | category | flops | bytes accessed | tf_op | source)
XLA Modules:
  0.0 38.3 jit_solution(9417218062106885195)
XLA Ops:
  0.0 36.3 %shard_map.55 = bf16[8,288,128]{2,1,0:T(8,128)(2,1)} custom-call(bf16[8,288,128]{2,1,0:T(8,128)(2,1)} %bitcast.7, bf16[1152,288]{1,0:T(8,128)(2,1)} %bitcast.6, bf16[8,2048]{1,0:T(8,128)(2,1)} %phonon_hbm.1, s32[1,8]{1,0:T(1,128)} %bitcast.9, s32[4,8]{1,0:T(4,128)} %bitcast.8), custom_call_target="tpu_custom_call" | custom-call | tf_op jit(solution)/shard_map/pallas_call | solution.py:215
  36.3 1.9 %copy.7 = bf16[128,8,288]{0,2,1:T(8,128)(2,1)} copy(bf16[128,8,288]{0,2,1:T(8,128)(2,1)} %bitcast.5) | data formatting | bytes 1179648

commit v4 on v3

--- a/solution.py
+++ b/solution.py
@@ -13,7 +13,7 @@
 BF16 = jnp.bfloat16
 
 
-def chunks_of(comps, step=96):
+def chunks_of(comps, step=112):
     return [(at, min(step, comps - at)) for at in range(0, comps, step)]
 
 

time: 38.4 us -> 38.4 us (level)
  no operation moved by 1% of the time
where the time goes in v4:
time: 38.4 us; the launch traced here: 38.3 us
  Pallas kernels  36.4 us (95%)
  local copies, waits for them, and re-layouts  1.92 us (5%)
    pallas_call x1, Pallas kernels, per_device(): pl.pallas_call(functools.partial(kernel, parts, groups), out_shape=jax.Sh...  36.4 us
    unnamed x1, local copies, waits for them, and re-layouts  1.92 us

profile of v4, /device:TPU:1, one launch (start us, length us, event | category | flops | bytes accessed | tf_op | source)
XLA Modules:
  0.0 38.3 jit_solution(16433305153260547526)
XLA Ops:
  0.0 36.4 %shard_map.55 = bf16[8,288,128]{2,1,0:T(8,128)(2,1)} custom-call(bf16[8,288,128]{2,1,0:T(8,128)(2,1)} %bitcast.7, bf16[1152,288]{1,0:T(8,128)(2,1)} %bitcast.6, bf16[8,2048]{1,0:T(8,128)(2,1)} %phonon_hbm.1, s32[1,8]{1,0:T(1,128)} %bitcast.9, s32[4,8]{1,0:T(4,128)} %bitcast.8), custom_call_target="tpu_custom_call" | custom-call | tf_op jit(solution)/shard_map/pallas_call | solution.py:215
  36.4 1.9 %copy.7 = bf16[128,8,288]{0,2,1:T(8,128)(2,1)} copy(bf16[128,8,288]{0,2,1:T(8,128)(2,1)} %bitcast.5) | data formatting | bytes 1179648
